TPU v7x, 32 devices: a whole 2x2x4 slice. The times are simulated.
32 devices in a mesh: seq: 8 (over y, x, core), tensor: 4 (over z).
Axes of the slice: x: 2, y: 2, z: 4, core: 2. Of those that a mesh axis runs over, the one named last changes fastest.
Arguments:
- tokens: bfloat16 [2048, 8192], P('seq', 'tensor'), may hold values from -24 to 24
- cotangent: bfloat16 [2048, 8192], P('seq', 'tensor'), may hold values from -6 to 6
- w_query: bfloat16 [8192, 4096], P(None, 'tensor'), may hold values from -1 to 1
- w_key: bfloat16 [8192, 1024], P(None, 'tensor'), may hold values from -1 to 1
- w_value: bfloat16 [8192, 1024], P(None, 'tensor'), may hold values from -0.0625 to 0.0625
- w_output: bfloat16 [4096, 8192], P('tensor'), may hold values from -0.09375 to 0.09375
- segments: int32 [2048], replicated, may hold values from 0 to 7, never falling along the last dimension, each value on 1 to 1024 neighbouring positions
- band: int32 [1], replicated, may hold values from 0 to 2047
Outputs:
- layer_out: bfloat16 [2048, 8192], P('seq', 'tensor')
- grad_tokens: bfloat16 [2048, 8192], P('seq', 'tensor')
- grad_query: float32 [8192, 4096], P('seq', 'tensor')
- grad_key: float32 [8192, 1024], P('seq', 'tensor')
- grad_value: float32 [8192, 1024], P('seq', 'tensor')
- grad_output: float32 [4096, 8192], P('tensor', 'seq')
All inputs are finite; a program needn't handle non-finite values.
Results may differ from a plain program's by a relative error of at most 0.025.
The roundings to bfloat16 on the way count: a program that leaves them out, or rounds other values in their place, can miss the bound.
Values may be sent and summed in bfloat16 or wider, within the bound.
A program may use at most 320 MiB of HBM per device.

v0:
```python
import math
import jax
import jax.numpy as jnp
from jax import lax
from jax.sharding import PartitionSpec as P

HD = 128


def tables(positions, width):
    half = width // 2
    freq = jnp.exp(-math.log(10000.0) * jnp.arange(half, dtype=jnp.float32) * 2.0 / width)
    angles = positions[:, None] * freq[None, :]
    return (jnp.cos(angles), jnp.sin(angles))


def rotate(values, cosine, sine, width):
    shaped = values.reshape(values.shape[0], -1, width)
    half = width // 2
    first = shaped[..., :half]
    second = shaped[..., half:]
    cos_b = cosine[:, None, :]
    sin_b = sine[:, None, :]
    turned = jnp.concatenate([first * cos_b - second * sin_b, second * cos_b + first * sin_b], -1)
    return turned.reshape(values.shape)


def rotate_back(values, cosine, sine, width):
    shaped = values.reshape(values.shape[0], -1, width)
    half = width // 2
    first = shaped[..., :half]
    second = shaped[..., half:]
    cos_b = cosine[:, None, :]
    sin_b = sine[:, None, :]
    turned = jnp.concatenate([first * cos_b + second * sin_b, second * cos_b - first * sin_b], -1)
    return turned.reshape(values.shape)


def contract_last(left, right):
    return lax.dot_general(
        left, right, (((1,), (1,)), ((), ())), preferred_element_type=jnp.float32
    )


def contract_first(left, right):
    return lax.dot_general(
        left, right, (((0,), (0,)), ((), ())), preferred_element_type=jnp.float32
    )


def swap(value, step):
    count = lax.axis_size("seq")
    return lax.ppermute(value, "seq", [(i, i ^ step) for i in range(count)])


def block_order(count):
    return list(range(0, count, 2)) + list(range(1, count, 2))


def gather_blocks(value):
    count = lax.axis_size("seq")
    even = [value] + [swap(value, step) for step in range(2, count, 2)]
    odd = [swap(piece, 1) for piece in even]
    return even + odd


def scatter_sum(pieces):
    f32 = jnp.float32
    half = len(pieces) // 2
    given = [swap(piece.astype(jnp.bfloat16), 1) for piece in pieces[half:]]
    paired = [pieces[k].astype(f32) + given[k].astype(f32) for k in range(half)]
    total = paired[0]
    for k in range(1, half):
        total = total + swap(paired[k].astype(jnp.bfloat16), 2 * k).astype(f32)
    return total


def reshard_columns(full):
    return lax.all_to_all(full, "seq", 1, 0, tiled=True)


def in_order(pieces, me):
    count = len(pieces)
    rows, columns = pieces[0].shape
    whole = jnp.zeros((count * rows, columns), pieces[0].dtype)
    for piece, step in zip(pieces, block_order(count)):
        whole = lax.dynamic_update_slice(whole, piece, ((me ^ step) * rows, 0))
    return whole


def after(value, *earlier):
    return lax.optimization_barrier((value, *earlier))[0]


def on_device(tokens, cotangent, w_query, w_key, w_value, w_output, segments, band):
    f32 = jnp.float32
    bf16 = jnp.bfloat16
    factor = 1.0 / math.sqrt(HD)
    tok_rows = tokens.shape[0]
    seq_count = lax.axis_size("seq")
    all_rows = tok_rows * seq_count
    q_width = w_query.shape[1]
    k_width = w_key.shape[1]
    kv_local = k_width // HD
    group = q_width // k_width
    me = lax.axis_index("seq")
    order = block_order(seq_count)
    full_x = lax.all_gather(tokens, "tensor", axis=1, tiled=True)
    full_grad = lax.all_gather(after(cotangent, full_x), "tensor", axis=1, tiled=True)
    first_row = me * tok_rows
    own_rows = first_row + jnp.arange(tok_rows)
    cosine, sine = tables(own_rows.astype(f32), HD)
    proj_k = jnp.dot(full_x, w_key, preferred_element_type=f32)
    proj_v = jnp.dot(full_x, w_value, preferred_element_type=f32)
    keys_local = rotate(proj_k, cosine, sine, HD).astype(bf16)
    values_local = proj_v.astype(bf16)
    kv_pieces = gather_blocks(jnp.concatenate([keys_local, values_local], 1))
    kv_all = jnp.concatenate(kv_pieces, 0)
    keys, values = (kv_all[:, :k_width], kv_all[:, k_width:])
    proj_q = jnp.dot(full_x, w_query, preferred_element_type=f32)
    query = rotate(proj_q, cosine, sine, HD).astype(bf16)
    x_cols = reshard_columns(full_x)
    key_rows = jnp.concatenate([(me ^ step) * tok_rows + jnp.arange(tok_rows) for step in order])
    key_seg = jnp.concatenate(
        [lax.dynamic_slice_in_dim(segments, (me ^ step) * tok_rows, tok_rows) for step in order]
    )
    own_seg = lax.dynamic_slice_in_dim(segments, first_row, tok_rows)
    allowed = (own_seg[:, None] == key_seg[None, :]) & (
        key_rows[None, :] <= own_rows[:, None] + band[0]
    )
    query4 = query.reshape(tok_rows, kv_local, group, HD)
    keys3 = keys.reshape(all_rows, kv_local, HD)
    values3 = values.reshape(all_rows, kv_local, HD)
    scores = jnp.einsum("igrd,jgd->grij", query4, keys3, preferred_element_type=f32) * factor
    masked = jnp.where(allowed[None, None], scores, -1e30)
    top = jnp.max(masked, -1, keepdims=True)
    expo = jnp.exp(masked - top)
    attend = expo / jnp.sum(expo, -1, keepdims=True)
    attend_b = attend.astype(bf16)
    heads4 = jnp.einsum("grij,jgd->igrd", attend_b, values3, preferred_element_type=f32).astype(
        bf16
    )
    heads = heads4.reshape(tok_rows, -1)
    out_part = jnp.dot(heads, w_output, preferred_element_type=f32).astype(bf16)
    layer_out = lax.psum_scatter(out_part, "tensor", scatter_dimension=1, tiled=True)
    full_grad = after(full_grad, out_part)
    g_cols = reshard_columns(full_grad)
    heads_all = in_order(gather_blocks(heads), me)
    grad_heads = after(contract_last(full_grad, w_output).astype(bf16), x_cols)
    grad4 = grad_heads.reshape(tok_rows, kv_local, group, HD)
    delta = jnp.sum(grad4.astype(f32) * heads4.astype(f32), -1).transpose(1, 2, 0)
    dprob = jnp.einsum("igrd,jgd->grij", grad4, values3, preferred_element_type=f32)
    score_grad = (attend * (dprob - delta[..., None])).astype(bf16)
    query_grad = (
        jnp.einsum("grij,jgd->igrd", score_grad, keys3, preferred_element_type=f32) * factor
    )
    key_part = jnp.einsum("grij,igrd->jgd", score_grad, query4, preferred_element_type=f32) * factor
    value_part = jnp.einsum("grij,igrd->jgd", attend_b, grad4, preferred_element_type=f32)
    kv_part = jnp.concatenate(
        [key_part.reshape(all_rows, -1), value_part.reshape(all_rows, -1)], 1
    ).astype(bf16)
    kv_part = after(kv_part, g_cols)
    kv_grad = scatter_sum([kv_part[k * tok_rows : (k + 1) * tok_rows] for k in range(seq_count)])
    pre_q = rotate_back(query_grad.reshape(tok_rows, -1), cosine, sine, HD).astype(bf16)
    pre_k = rotate_back(kv_grad[:, :k_width], cosine, sine, HD).astype(bf16)
    pre_v = kv_grad[:, k_width:].astype(bf16)
    grad_part = (
        contract_last(pre_q, w_query) + contract_last(pre_k, w_key) + contract_last(pre_v, w_value)
    ).astype(bf16)
    grad_tokens = lax.psum_scatter(grad_part, "tensor", scatter_dimension=1, tiled=True)
    pre_cat = after(jnp.concatenate([pre_q, pre_k, pre_v], 1), heads_all)
    pre_all = in_order(gather_blocks(pre_cat), me)
    grad_output = contract_first(heads_all, g_cols)
    merged = contract_first(x_cols, pre_all)
    grad_query = merged[:, :q_width]
    grad_key = merged[:, q_width : q_width + k_width]
    grad_value = merged[:, q_width + k_width :]
    return (layer_out, grad_tokens, grad_query, grad_key, grad_value, grad_output)


def solution(mesh):
    in_specs = (
        P("seq", "tensor"),
        P("seq", "tensor"),
        P(None, "tensor"),
        P(None, "tensor"),
        P(None, "tensor"),
        P("tensor", None),
        P(),
        P(),
    )
    out_specs = (
        P("seq", "tensor"),
        P("seq", "tensor"),
        P("seq", "tensor"),
        P("seq", "tensor"),
        P("seq", "tensor"),
        P("tensor", "seq"),
    )
    return jax.shard_map(
        on_device, mesh=mesh, in_specs=in_specs, out_specs=out_specs, check_vma=False
    )
```

profile of v0, /device:TPU:0, one launch (start us, length us, event | category | flops | bytes accessed | tf_op | source)
XLA Modules:
  0.0 408.1 jit_solution(2995070585059447947)
XLA Ops:
  18.5 75.2 %all-gather.3.cloned.1.call-done = bf16[256,8192]{0,1:T(8,128)(2,1)} async-done(((bf16[256,2048]{0,1:T(8,128)(2,1)}), bf16[256,8192]{0,1:T(8,128)(2,1)}) %all-gather.3.cloned.1.call-update) | async-done | bytes 4194320 | tf_op jit(solution)/shard_map/all_gather | solution.py:108
  93.6 5.3 %fusion.25 = f32[256,256]{0,1:T(8,128)S(1)} fusion(bf16[256,8192]{0,1:T(8,128)(2,1)} %all-gather.3.cloned.1.call-done, bf16[8192,256]{1,0:T(8,128)(2,1)} %param.11), kind=kOutput, calls=%fused_computation.106 | convolution fusion | flops 1073741824 | bytes 8650752 | tf_op jit(solution)/shard_map/dot_general | solution.py:113
  99.0 5.9 %convolution_convert_fusion.3 = bf16[256,256]{0,1:T(8,128)(2,1)S(1)} fusion(bf16[256,8192]{0,1:T(8,128)(2,1)} %all-gather.3.cloned.1.call-done, bf16[8192,256]{1,0:T(8,128)(2,1)} %param.12), kind=kOutput, calls=%fused_computation.29 | convolution fusion | flops 1073807360 | bytes 8519680 | tf_op jit(solution)/shard_map/dot_general | solution.py:114
  109.3 6.5 %convolution_bitcast_fusion.3 = f32[32,8,8,128]{3,1,2,0:T(8,128)S(1)} fusion(bf16[256,8192]{0,1:T(8,128)(2,1)} %all-gather.3.cloned.1.call-done, bf16[8192,1024]{1,0:T(8,128)(2,1)S(1)} %copy-done), kind=kOutput, calls=%fused_computation.25 | convolution fusion | flops 4294967296 | bytes 22020096 | tf_op jit(solution)/shard_map/dot_general | solution.py:120
  118.2 4.5 %all-to-all-start = ((bf16[256,8,1024]{0,2,1:T(8,128)(2,1)}), bf16[256,8,1024]{0,2,1:T(8,128)(2,1)}, u32[]{:S(2)}, u32[]{:S(2)}) async-start(bf16[256,8,1024]{0,2,1:T(8,128)(2,1)} %bitcast.118), calls=%async_computation.1 | async-start | bytes 8388608 | tf_op jit(solution)/shard_map/all_to_all | solution.py:79
  134.7 9.4 %fusion.23 = (f32[2,4,256]{2,1,0:T(4,128)S(1)}, f32[2,4,256,2048]{2,3,1,0:T(8,128)}) fusion(pred[256,2048]{0,1:T(8,128)(4,1)S(1)} %compare_and_fusion, bf16[2048,2,128,1]{0,2,3,1:T(8,128)(2,1)S(1)} %bitcast.136, bf16[256,2,4,128]{3,0,2,1:T(8,128)(2,1)S(1)} %bitcast.142), kind=kOutput, calls=%fused_computation.104 | convolution fusion | flops 1090521088 | bytes 18882560 | tf_op jit(solution)/shard_map/sub | solution.py:137
  144.1 7.4 %fusion.8 = bf16[2,4,256,2048]{2,3,1,0:T(8,128)(2,1)S(1)} fusion(f32[2,4,256,2048]{2,3,1,0:T(8,128)} %get-tuple-element.62, f32[2,4,256]{2,1,0:T(4,128)S(1)} %get-tuple-element.61), kind=kLoop, calls=%fused_computation.15 | loop fusion | flops 8388608 | bytes 25174016 | tf_op jit(solution)/shard_map/convert_element_type | solution.py:139
  152.8 3.0 copy-done.1
  158.1 6.4 %convolution_convert_fusion = bf16[256,8192]{1,0:T(8,128)(2,1)} fusion(bf16[256,1024]{0,1:T(8,128)(2,1)S(1)} %bitcast.122, bf16[1024,8192]{1,0:T(8,128)(2,1)S(1)} %bitcast.120), kind=kOutput, calls=%fused_computation.9 | convolution fusion | flops 4297064448 | bytes 21495808 | tf_op jit(solution)/shard_map/dot_general | solution.py:144
  164.6 7.3 %all-to-all-done = bf16[256,8,1024]{0,2,1:T(8,128)(2,1)} async-done(((bf16[256,8,1024]{0,2,1:T(8,128)(2,1)}), bf16[256,8,1024]{0,2,1:T(8,128)(2,1)}, u32[]{:S(2)}, u32[]{:S(2)}) %all-to-all-start) | async-done | bytes 4194336 | tf_op jit(solution)/shard_map/all_to_all | solution.py:79
  171.9 6.4 %copy.59 = bf16[8,256,1024]{2,1,0:T(8,128)(2,1)} copy(bf16[8,256,1024]{1,2,0:T(8,128)(2,1)} %bitcast.16) | data formatting | bytes 8388608 | tf_op jit(solution)/shard_map/all_to_all | solution.py:79
  178.3 18.7 %all-gather.5.cloned.1.call-done = bf16[256,8192]{0,1:T(8,128)(2,1)} async-done(((bf16[256,2048]{0,1:T(8,128)(2,1)}), bf16[256,8192]{0,1:T(8,128)(2,1)}) %all-gather.5.cloned.1.call-update) | async-done | bytes 4194320 | tf_op jit(solution)/shard_map/all_gather | solution.py:109
  196.9 11.6 %convolution_convert_fusion.2 = bf16[256,1024]{1,0:T(8,128)(2,1)S(1)} fusion(bf16[256,8192]{0,1:T(8,128)(2,1)} %all-gather.5.cloned.1.call-done, bf16[1024,8192]{1,0:T(8,128)(2,1)} %param.13), kind=kOutput, calls=%fused_computation.28 | convolution fusion | flops 4295229440 | bytes 21495808 | tf_op jit(solution)/shard_map/dot_general | solution.py:40
  208.9 4.6 %all-to-all-start.1 = ((bf16[256,8,1024]{0,2,1:T(8,128)(2,1)}), bf16[256,8,1024]{0,2,1:T(8,128)(2,1)}, u32[]{:S(2)}, u32[]{:S(2)}) async-start(bf16[256,8,1024]{0,2,1:T(8,128)(2,1)} %bitcast.135), calls=%async_computation.2 | async-start | bytes 8388608 | tf_op jit(solution)/shard_map/all_to_all | solution.py:79
  213.5 8.0 %fusion.2 = bf16[2,4,256,2048]{2,3,1,0:T(8,128)(2,1)S(1)} fusion(f32[2,4,256]{2,1,0:T(4,128)S(1)} %bitcast.150, f32[2,4,256,2048]{2,3,1,0:T(8,128)} %get-tuple-element.62, f32[2,4,256]{2,1,0:T(4,128)S(1)} %get-tuple-element.61, bf16[2048,2,128,1]{0,2,3,1:T(8,128)(2,1)} %bitcast.139, bf16[256,2,4,128]{0,3,2,1:T(8,128)(2,1)S(1)} %bitcast.130), kind=kOutput, calls=%fused_computation.3 | convolution fusion | flops 1090519040 | bytes 26755072 | tf_op jit(solution)/shard_map/igrd,jgd->grij/dot_general | solution.py:152
  221.5 3.3 convolution_multiply_fusion
  227.6 6.3 %fusion.13 = bf16[2,128,2048]{2,1,0:T(8,128)(2,1)S(1)} fusion(bf16[256,2,4,128]{0,3,2,1:T(8,128)(2,1)S(1)} %bitcast.131, bf16[2,4,256,2048]{2,3,1,0:T(8,128)(2,1)} %copy-done.1), kind=kOutput, calls=%fused_computation.22 | convolution fusion | flops 1074266112 | bytes 9961472 | tf_op jit(solution)/shard_map/grij,igrd->jgd/dot_general | solution.py:158
  233.9 2.9 fusion.12
  237.1 25.6 %all-to-all-done.1 = bf16[256,8,1024]{0,2,1:T(8,128)(2,1)} async-done(((bf16[256,8,1024]{0,2,1:T(8,128)(2,1)}), bf16[256,8,1024]{0,2,1:T(8,128)(2,1)}, u32[]{:S(2)}, u32[]{:S(2)}) %all-to-all-start.1) | async-done | bytes 4194336 | tf_op jit(solution)/shard_map/all_to_all | solution.py:79
  262.6 6.4 %copy.69 = bf16[8,256,1024]{2,1,0:T(8,128)(2,1)} copy(bf16[8,256,1024]{1,2,0:T(8,128)(2,1)} %bitcast.35) | data formatting | bytes 8388608 | tf_op jit(solution)/shard_map/all_to_all | solution.py:79
  277.5 19.2 %fusion.18 = f32[256,8192]{1,0:T(8,128)} fusion(bf16[8192,1024]{1,0:T(8,128)(2,1)} %param.10, bf16[32,8,8,128]{3,2,1,0:T(8,128)(2,1)S(1)} %bitcast.128), kind=kOutput, calls=%fused_computation.99 | convolution fusion | flops 4294967296 | bytes 25690112 | tf_op jit(solution)/shard_map/dot_general | solution.py:40
  298.2 6.1 %convolution_add_fusion.1 = f32[256,8192]{1,0:T(8,128)S(1)} fusion(f32[256,8192]{1,0:T(8,128)} %fusion.18, bf16[256,256]{0,1:T(8,128)(2,1)S(1)} %bitcast.145, bf16[8192,256]{1,0:T(8,128)(2,1)} %param.11), kind=kOutput, calls=%fused_computation.8 | convolution fusion | flops 1075838976 | bytes 21102592 | tf_op jit(solution)/shard_map/dot_general | solution.py:40
  304.3 3.3 fusion.4
  311.1 11.4 %collective-permute-done.14 = bf16[256,1024]{0,1:T(8,128)(2,1)S(1)} collective-permute-done((bf16[256,1024]{0,1:T(8,128)(2,1)S(1)}, bf16[256,1024]{0,1:T(8,128)(2,1)S(1)}, u32[]{:S(2)}, u32[]{:S(2)}) %collective-permute-start.14) | collective-permute-done | bytes 524320 | tf_op jit(solution)/shard_map/ppermute | solution.py:53
  323.1 9.1 %collective-permute-done.15 = bf16[256,1024]{0,1:T(8,128)(2,1)S(1)} collective-permute-done((bf16[256,1024]{0,1:T(8,128)(2,1)S(1)}, bf16[256,1024]{0,1:T(8,128)(2,1)S(1)}, u32[]{:S(2)}, u32[]{:S(2)}) %collective-permute-start.15) | collective-permute-done | bytes 524320 | tf_op jit(solution)/shard_map/ppermute | solution.py:53
  341.7 10.0 %fusion.26 = f32[1024,1024]{1,0:T(8,128)} fusion(bf16[2048,1024]{0,1:T(8,128)(2,1)} %copy-done.6, bf16[2048,1024]{1,0:T(8,128)(2,1)} %bitcast.134), kind=kOutput, calls=%fused_computation.107 | convolution fusion | flops 4294967296 | bytes 12582912 | tf_op jit(solution)/shard_map/dot_general | solution.py:46
  352.1 6.4 %collective-permute-done.21 = bf16[256,1536]{1,0:T(8,128)(2,1)S(1)} collective-permute-done((bf16[256,1536]{1,0:T(8,128)(2,1)S(1)}, bf16[256,1536]{1,0:T(8,128)(2,1)S(1)}, u32[]{:S(2)}, u32[]{:S(2)}) %collective-permute-start.21) | collective-permute-done | bytes 786464 | tf_op jit(solution)/shard_map/ppermute | solution.py:53
  358.6 17.2 %collective-permute-done.22 = bf16[256,1536]{1,0:T(8,128)(2,1)S(1)} collective-permute-done((bf16[256,1536]{1,0:T(8,128)(2,1)S(1)}, bf16[256,1536]{1,0:T(8,128)(2,1)S(1)}, u32[]{:S(2)}, u32[]{:S(2)}) %collective-permute-start.22) | collective-permute-done | bytes 786464 | tf_op jit(solution)/shard_map/ppermute | solution.py:53
  379.3 7.0 %convolution_bitcast_fusion = f32[1024,1536]{0,1:T(8,128)S(1)} fusion(bf16[2048,1536]{1,0:T(8,128)(2,1)S(1)} %constant_dynamic-update-slice_fusion.24, bf16[2048,1024]{1,0:T(8,128)(2,1)S(1)} %bitcast.133), kind=kOutput, calls=%fused_computation.16 | convolution fusion | flops 6442450944 | bytes 16777216 | tf_op jit(solution)/shard_map/dot_general | solution.py:46
  386.4 2.6 copy-done.4
  389.0 2.7 slice.105
  391.7 5.3 %copy.72 = f32[1024,1024]{1,0:T(8,128)} copy(f32[1024,1024]{0,1:T(8,128)} %slice.105) | data formatting | bytes 8388608
  (179 shorter events, 67.7 us)
Async XLA Ops:
  7.2 86.5 %all-gather.3.cloned.1.call-start = ((), (), s32[]{:S(2)}) async-start(), calls=%async_computation.4 | async-start | bytes 5242880 | tf_op jit(solution)/shard_map/all_gather | solution.py:108
  9.5 187.4 %all-gather.5.cloned.1.call-start = ((), (), s32[]{:S(2)}) async-start(), calls=%async_computation.6 | async-start | bytes 5242880 | tf_op jit(solution)/shard_map/all_gather | solution.py:109
  105.8 17.2 %collective-permute-start = (bf16[256,512]{0,1:T(8,128)(2,1)}, bf16[256,512]{0,1:T(8,128)(2,1)}, u32[]{:S(2)}, u32[]{:S(2)}) collective-permute-start(bf16[256,512]{0,1:T(8,128)(2,1)} %get-tuple-element.57), channel_id=1, source_target_pairs={{0,8},{4,12},{8,0},{12,4},{16,24},{20,28},{24,16},{28,20},{1,9},{5... | collective-permute-start | bytes 786440 | tf_op jit(solution)/shard_map/ppermute | solution.py:53
  107.3 17.9 %collective-permute-start.1 = (bf16[256,512]{0,1:T(8,128)(2,1)}, bf16[256,512]{0,1:T(8,128)(2,1)}, u32[]{:S(2)}, u32[]{:S(2)}) collective-permute-start(bf16[256,512]{0,1:T(8,128)(2,1)} %get-tuple-element.57), channel_id=1, source_target_pairs={{0,16},{4,20},{8,24},{12,28},{16,0},{20,4},{24,8},{28,12},{1,17},{... | collective-permute-start | bytes 786440 | tf_op jit(solution)/shard_map/ppermute | solution.py:53
  108.8 18.2 %collective-permute-start.2 = (bf16[256,512]{0,1:T(8,128)(2,1)}, bf16[256,512]{0,1:T(8,128)(2,1)}, u32[]{:S(2)}, u32[]{:S(2)}) collective-permute-start(bf16[256,512]{0,1:T(8,128)(2,1)} %get-tuple-element.57), channel_id=1, source_target_pairs={{0,24},{4,28},{8,16},{12,20},{16,8},{20,12},{24,0},{28,4},{1,25},{... | collective-permute-start | bytes 786440 | tf_op jit(solution)/shard_map/ppermute | solution.py:53
  109.3 19.8 %collective-permute-start.3 = (bf16[256,512]{0,1:T(8,128)(2,1)}, bf16[256,512]{0,1:T(8,128)(2,1)}, u32[]{:S(2)}, u32[]{:S(2)}) collective-permute-start(bf16[256,512]{0,1:T(8,128)(2,1)} %get-tuple-element.57), channel_id=1, source_target_pairs={{0,4},{4,0},{8,12},{12,8},{16,20},{20,16},{24,28},{28,24},{1,5},{5... | collective-permute-start | bytes 786440 | tf_op jit(solution)/shard_map/ppermute | solution.py:53
  118.2 53.7 %all-to-all-start = ((bf16[256,8,1024]{0,2,1:T(8,128)(2,1)}), bf16[256,8,1024]{0,2,1:T(8,128)(2,1)}, u32[]{:S(2)}, u32[]{:S(2)}) async-start(bf16[256,8,1024]{0,2,1:T(8,128)(2,1)} %bitcast.118), calls=%async_computation.1 | async-start | bytes 8388608 | tf_op jit(solution)/shard_map/all_to_all | solution.py:79
  122.7 278.6 %reduce-scatter.3.cloned.1.call-start = ((), (), s32[]{:S(2)}) async-start(), calls=%async_computation.5 | async-start | bytes 5242880 | tf_op jit(solution)/shard_map/reduce_scatter | solution.py:145
  123.0 7.8 %collective-permute-start.4 = (bf16[256,512]{0,1:T(8,128)(2,1)}, bf16[256,512]{0,1:T(8,128)(2,1)S(1)}, u32[]{:S(2)}, u32[]{:S(2)}) collective-permute-start(bf16[256,512]{0,1:T(8,128)(2,1)} %collective-permute-done), channel_id=1, source_target_pairs={{0,4},{4,0},{8,12},{12,8},{16,20},{20,16},{24,28},{28,24},{1,5},{5... | collective-permute-start | bytes 786440 | tf_op jit(solution)/shard_map/ppermute | solution.py:53
  125.2 6.3 %collective-permute-start.5 = (bf16[256,512]{0,1:T(8,128)(2,1)}, bf16[256,512]{0,1:T(8,128)(2,1)S(1)}, u32[]{:S(2)}, u32[]{:S(2)}) collective-permute-start(bf16[256,512]{0,1:T(8,128)(2,1)} %collective-permute-done.1), channel_id=1, source_target_pairs={{0,4},{4,0},{8,12},{12,8},{16,20},{20,16},{24,28},{28,24},{1,5},{5... | collective-permute-start | bytes 786440 | tf_op jit(solution)/shard_map/ppermute | solution.py:53
  127.0 5.3 %collective-permute-start.6 = (bf16[256,512]{0,1:T(8,128)(2,1)}, bf16[256,512]{0,1:T(8,128)(2,1)S(1)}, u32[]{:S(2)}, u32[]{:S(2)}) collective-permute-start(bf16[256,512]{0,1:T(8,128)(2,1)} %collective-permute-done.2), channel_id=1, source_target_pairs={{0,4},{4,0},{8,12},{12,8},{16,20},{20,16},{24,28},{28,24},{1,5},{5... | collective-permute-start | bytes 786440 | tf_op jit(solution)/shard_map/ppermute | solution.py:53
  208.9 53.7 %all-to-all-start.1 = ((bf16[256,8,1024]{0,2,1:T(8,128)(2,1)}), bf16[256,8,1024]{0,2,1:T(8,128)(2,1)}, u32[]{:S(2)}, u32[]{:S(2)}) async-start(bf16[256,8,1024]{0,2,1:T(8,128)(2,1)} %bitcast.135), calls=%async_computation.2 | async-start | bytes 8388608 | tf_op jit(solution)/shard_map/all_to_all | solution.py:79
  213.5 187.8 %reduce-scatter.5.cloned.1.call-start = ((), (), s32[]{:S(2)}) async-start(), calls=%async_computation.7 | async-start | bytes 5242880 | tf_op jit(solution)/shard_map/reduce_scatter | solution.py:170
  269.8 3.2 collective-permute-start.8
  269.8 3.2 collective-permute-start.12
  270.3 2.7 collective-permute-start.10
  272.5 24.3 %collective-permute-start.7 = (bf16[256,512]{0,1:T(8,128)(2,1)}, bf16[256,512]{0,1:T(8,128)(2,1)S(1)}, u32[]{:S(2)}, u32[]{:S(2)}) collective-permute-start(bf16[256,512]{0,1:T(8,128)(2,1)} %get-tuple-element.40), channel_id=1, source_target_pairs={{0,4},{4,0},{8,12},{12,8},{16,20},{20,16},{24,28},{28,24},{1,5},{5... | collective-permute-start | bytes 786440 | tf_op jit(solution)/shard_map/ppermute | solution.py:53
  274.1 22.7 %collective-permute-start.13 = (bf16[256,512]{0,1:T(8,128)(2,1)}, bf16[256,512]{0,1:T(8,128)(2,1)}, u32[]{:S(2)}, u32[]{:S(2)}) collective-permute-start(bf16[256,512]{0,1:T(8,128)(2,1)} %get-tuple-element.45), channel_id=1, source_target_pairs={{0,24},{4,28},{8,16},{12,20},{16,8},{20,12},{24,0},{28,4},{1,25},{... | collective-permute-start | bytes 786440 | tf_op jit(solution)/shard_map/ppermute | solution.py:53
  274.7 22.1 %collective-permute-start.11 = (bf16[256,512]{0,1:T(8,128)(2,1)}, bf16[256,512]{0,1:T(8,128)(2,1)}, u32[]{:S(2)}, u32[]{:S(2)}) collective-permute-start(bf16[256,512]{0,1:T(8,128)(2,1)} %get-tuple-element.46), channel_id=1, source_target_pairs={{0,16},{4,20},{8,24},{12,28},{16,0},{20,4},{24,8},{28,12},{1,17},{... | collective-permute-start | bytes 786440 | tf_op jit(solution)/shard_map/ppermute | solution.py:53
  276.0 20.7 %collective-permute-start.9 = (bf16[256,512]{0,1:T(8,128)(2,1)}, bf16[256,512]{0,1:T(8,128)(2,1)}, u32[]{:S(2)}, u32[]{:S(2)}) collective-permute-start(bf16[256,512]{0,1:T(8,128)(2,1)} %get-tuple-element.44), channel_id=1, source_target_pairs={{0,8},{4,12},{8,0},{12,4},{16,24},{20,28},{24,16},{28,20},{1,9},{5... | collective-permute-start | bytes 786440 | tf_op jit(solution)/shard_map/ppermute | solution.py:53
  307.6 14.9 %collective-permute-start.14 = (bf16[256,1024]{0,1:T(8,128)(2,1)S(1)}, bf16[256,1024]{0,1:T(8,128)(2,1)S(1)}, u32[]{:S(2)}, u32[]{:S(2)}) collective-permute-start(bf16[256,1024]{0,1:T(8,128)(2,1)S(1)} %bitcast.123), channel_id=1, source_target_pairs={{0,8},{4,12},{8,0},{12,4},{16,24},{20,28},{24,16},{28,20},{1,9},{5... | collective-permute-start | bytes 1572872 | tf_op jit(solution)/shard_map/ppermute | solution.py:53
  308.1 24.0 %collective-permute-start.15 = (bf16[256,1024]{0,1:T(8,128)(2,1)S(1)}, bf16[256,1024]{0,1:T(8,128)(2,1)S(1)}, u32[]{:S(2)}, u32[]{:S(2)}) collective-permute-start(bf16[256,1024]{0,1:T(8,128)(2,1)S(1)} %bitcast.124), channel_id=1, source_target_pairs={{0,16},{4,20},{8,24},{12,28},{16,0},{20,4},{24,8},{28,12},{1,17},{... | collective-permute-start | bytes 1572872 | tf_op jit(solution)/shard_map/ppermute | solution.py:53
  308.8 23.4 %collective-permute-start.16 = (bf16[256,1024]{0,1:T(8,128)(2,1)S(1)}, bf16[256,1024]{0,1:T(8,128)(2,1)S(1)}, u32[]{:S(2)}, u32[]{:S(2)}) collective-permute-start(bf16[256,1024]{0,1:T(8,128)(2,1)S(1)} %bitcast.125), channel_id=1, source_target_pairs={{0,24},{4,28},{8,16},{12,20},{16,8},{20,12},{24,0},{28,4},{1,25},{... | collective-permute-start | bytes 1572872 | tf_op jit(solution)/shard_map/ppermute | solution.py:53
  311.1 21.8 %collective-permute-start.17 = (bf16[256,1024]{0,1:T(8,128)(2,1)S(1)}, bf16[256,1024]{0,1:T(8,128)(2,1)S(1)}, u32[]{:S(2)}, u32[]{:S(2)}) collective-permute-start(bf16[256,1024]{0,1:T(8,128)(2,1)S(1)} %bitcast.126), channel_id=1, source_target_pairs={{0,4},{4,0},{8,12},{12,8},{16,20},{20,16},{24,28},{28,24},{1,5},{5... | collective-permute-start | bytes 1572872 | tf_op jit(solution)/shard_map/ppermute | solution.py:53
  322.5 10.6 %collective-permute-start.18 = (bf16[256,1024]{0,1:T(8,128)(2,1)S(1)}, bf16[256,1024]{0,1:T(8,128)(2,1)S(1)}, u32[]{:S(2)}, u32[]{:S(2)}) collective-permute-start(bf16[256,1024]{0,1:T(8,128)(2,1)S(1)} %collective-permute-done.14), channel_id=1, source_target_pairs={{0,4},{4,0},{8,12},{12,8},{16,20},{20,16},{24,28},{28,24},{1,5},{5... | collective-permute-start | bytes 1572872 | tf_op jit(solution)/shard_map/ppermute | solution.py:53
  332.2 2.6 collective-permute-start.20
  338.1 20.4 %collective-permute-start.21 = (bf16[256,1536]{1,0:T(8,128)(2,1)S(1)}, bf16[256,1536]{1,0:T(8,128)(2,1)S(1)}, u32[]{:S(2)}, u32[]{:S(2)}) collective-permute-start(bf16[256,1536]{1,0:T(8,128)(2,1)S(1)} %pad_maximum_fusion.1), channel_id=1, source_target_pairs={{0,8},{4,12},{8,0},{12,4},{16,24},{20,28},{24,16},{28,20},{1,9},{5... | collective-permute-start | bytes 2359304 | tf_op jit(solution)/shard_map/ppermute | solution.py:53
  339.7 36.2 %collective-permute-start.22 = (bf16[256,1536]{1,0:T(8,128)(2,1)S(1)}, bf16[256,1536]{1,0:T(8,128)(2,1)S(1)}, u32[]{:S(2)}, u32[]{:S(2)}) collective-permute-start(bf16[256,1536]{1,0:T(8,128)(2,1)S(1)} %pad_maximum_fusion.1), channel_id=1, source_target_pairs={{0,16},{4,20},{8,24},{12,28},{16,0},{20,4},{24,8},{28,12},{1,17},{... | collective-permute-start | bytes 2359304 | tf_op jit(solution)/shard_map/ppermute | solution.py:53
  340.2 35.7 %collective-permute-start.23 = (bf16[256,1536]{1,0:T(8,128)(2,1)S(1)}, bf16[256,1536]{1,0:T(8,128)(2,1)S(1)}, u32[]{:S(2)}, u32[]{:S(2)}) collective-permute-start(bf16[256,1536]{1,0:T(8,128)(2,1)S(1)} %pad_maximum_fusion.1), channel_id=1, source_target_pairs={{0,24},{4,28},{8,16},{12,20},{16,8},{20,12},{24,0},{28,4},{1,25},{... | collective-permute-start | bytes 2359304 | tf_op jit(solution)/shard_map/ppermute | solution.py:53
  351.6 24.9 %collective-permute-start.24 = (bf16[256,1536]{1,0:T(8,128)(2,1)S(1)}, bf16[256,1536]{1,0:T(8,128)(2,1)S(1)}, u32[]{:S(2)}, u32[]{:S(2)}) collective-permute-start(bf16[256,1536]{1,0:T(8,128)(2,1)S(1)} %pad_maximum_fusion.1), channel_id=1, source_target_pairs={{0,4},{4,0},{8,12},{12,8},{16,20},{20,16},{24,28},{28,24},{1,5},{5... | collective-permute-start | bytes 2359304 | tf_op jit(solution)/shard_map/ppermute | solution.py:53
  358.6 18.1 %collective-permute-start.25 = (bf16[256,1536]{1,0:T(8,128)(2,1)S(1)}, bf16[256,1536]{1,0:T(8,128)(2,1)S(1)}, u32[]{:S(2)}, u32[]{:S(2)}) collective-permute-start(bf16[256,1536]{1,0:T(8,128)(2,1)S(1)} %collective-permute-done.21), channel_id=1, source_target_pairs={{0,4},{4,0},{8,12},{12,8},{16,20},{20,16},{24,28},{28,24},{1,5},{5... | collective-permute-start | bytes 2359304 | tf_op jit(solution)/shard_map/ppermute | solution.py:53
  375.9 3.3 collective-permute-start.27
  (20 other events, 156.0 us)
Sparse Core Ops, SparseCore 0:
  10.1 83.4 all-gather.2
  117.5 79.4 all-gather.4
  199.8 75.2 reduce-scatter.2
  307.7 73.5 reduce-scatter.4
where the time goes:
time: 416 us; the launch traced here: 408 us
  waiting for transfers between devices  175 us (42%)
  matrix products  112 us (27%)
  local copies, waits for them, and re-layouts  62.7 us (15%)
  starting transfers between devices  26.8 us (6%)
  other arithmetic  15.7 us (4%)
  between operations  15.5 us (4%)
    all_gather x1, waiting for transfers between devices, on_device(): full_x = lax.all_gather(tokens, 'tensor', axis=1, tiled=True)  75.2 us
    ppermute x28, waiting for transfers between devices, swap(): return lax.ppermute(value, 'seq', [(i, i ^ step) for i in range(count)])  48.2 us
    dot_general x4, matrix products, contract_last(): lax.dot_general(left, right, (((1,), (1,)), ((), ())), preferred_element_...  40.1 us
    unnamed x57, local copies, waits for them, and re-layouts  36.6 us
    all_to_all x2, waiting for transfers between devices, reshard_columns(): return lax.all_to_all(full, 'seq', 1, 0, tiled=True)  32.8 us
    all_gather x1, waiting for transfers between devices, on_device(): lax.all_gather(after(cotangent, full_x), 'tensor', axis=1, tiled=True)  18.7 us
    ppermute x28, starting transfers between devices, swap(): return lax.ppermute(value, 'seq', [(i, i ^ step) for i in range(count)])  17.4 us
    dot_general x2, matrix products, contract_first(): lax.dot_general(left, right, (((0,), (0,)), ((), ())), preferred_element_...  17 us
  transfers between devices with their start and end apart: 34, of which 12 were waited for; matrix products, arithmetic and copies ran while one was open for 41% of the time, Pallas kernels for 0%

commit v1 on v0

--- a/solution.py
+++ b/solution.py
@@ -5,6 +5,24 @@
 from jax.sharding import PartitionSpec as P
 
 HD = 128
+
+
+def joined_along(pieces, dim):
+    lengths = list(pieces.shape[1:])
+    lengths[dim] *= pieces.shape[0]
+    return jnp.moveaxis(pieces, 0, dim).reshape(lengths)
+
+
+def collected_by_bits(array, axis):
+    size = lax.axis_size(axis)
+    pieces = array[None]
+    for level in range(size.bit_length() - 1):
+        bit = 1 << level
+        other = lax.ppermute(pieces, axis, [(i, i ^ bit) for i in range(size)])
+        both = jnp.stack([pieces, other])
+        upper = lax.axis_index(axis) >> level & 1
+        pieces = jnp.where(upper == 0, both, both[::-1]).reshape(-1, *array.shape)
+    return pieces
 
 
 def tables(positions, width):
@@ -106,7 +124,8 @@
     me = lax.axis_index("seq")
     order = block_order(seq_count)
     full_x = lax.all_gather(tokens, "tensor", axis=1, tiled=True)
-    full_grad = lax.all_gather(after(cotangent, full_x), "tensor", axis=1, tiled=True)
+    array = after(cotangent, full_x)
+    full_grad = joined_along(collected_by_bits(array, "tensor"), 1)
     first_row = me * tok_rows
     own_rows = first_row + jnp.arange(tok_rows)
     cosine, sine = tables(own_rows.astype(f32), HD)

time: 416 us -> 538 us (1.29)
  waiting for transfers between devices: 175 us -> 285 us
  other arithmetic: 15.7 us -> 25.2 us
    ppermute x0 -> x2, waiting for transfers between devices: none -> 144 us  [collected_by_bits(): other = lax.ppermute(pieces, axis, [(i, i ^ bit) for i in range(size)])]
    all_gather x1 -> x0, waiting for transfers between devices: 18.7 us -> none  [on_device(): lax.all_gather(after(cotangent, full_x), 'tensor', axis=1, tiled=True)]
    all_to_all x2, waiting for transfers between devices: 32.8 us -> 19.1 us  [reshard_columns(): return lax.all_to_all(full, 'seq', 1, 0, tiled=True)]
    unnamed x57 -> x53, local copies, waits for them, and re-layouts: 36.6 us -> 29.2 us
    select_n x0 -> x1, local copies, waits for them, and re-layouts: none -> 6.18 us  [collected_by_bits(): pieces = jnp.where(upper == 0, both, both[::-1]).reshape(-1, *array.shape)]
    another operation x4 -> x7, other arithmetic: 2.34 us -> 8.16 us  [the longest x3 5.76 us: collected_by_bits(): both = jnp.stack([pieces, other])]
  transfers between devices with their start and end apart: 34 -> 35, of which waited for: 12 -> 13; matrix products, arithmetic and copies ran while one was open for 41% -> 33% of each run, Pallas kernels for 0% -> 0%
where the time goes in v1:
time: 538 us; the launch traced here: 530 us
  waiting for transfers between devices  285 us (53%)
  matrix products  116 us (22%)
  local copies, waits for them, and re-layouts  59.9 us (11%)
  starting transfers between devices  27.9 us (5%)
  other arithmetic  25.2 us (5%)
  between operations  15.8 us (3%)
    ppermute x2, waiting for transfers between devices, collected_by_bits(): other = lax.ppermute(pieces, axis, [(i, i ^ bit) for i in range(size)])  144 us
    all_gather x1, waiting for transfers between devices, on_device(): full_x = lax.all_gather(tokens, 'tensor', axis=1, tiled=True)  74.4 us
    ppermute x28, waiting for transfers between devices, swap(): return lax.ppermute(value, 'seq', [(i, i ^ step) for i in range(count)])  48.5 us
    dot_general x4, matrix products, contract_last(): lax.dot_general(left, right, (((1,), (1,)), ((), ())), preferred_element_...  40.3 us
    unnamed x53, local copies, waits for them, and re-layouts  29.2 us
    all_to_all x2, waiting for transfers between devices, reshard_columns(): return lax.all_to_all(full, 'seq', 1, 0, tiled=True)  19.1 us
    ppermute x28, starting transfers between devices, swap(): return lax.ppermute(value, 'seq', [(i, i ^ step) for i in range(count)])  17.5 us
    dot_general x2, matrix products, contract_first(): lax.dot_general(left, right, (((0,), (0,)), ((), ())), preferred_element_...  17.1 us
  transfers between devices with their start and end apart: 35, of which 13 were waited for; matrix products, arithmetic and copies ran while one was open for 33% of the time, Pallas kernels for 0%

profile of v1, /device:TPU:0, one launch (start us, length us, event | category | flops | bytes accessed | tf_op | source)
XLA Modules:
  0.0 529.9 jit_solution(17396929227339679512)
XLA Ops:
  19.3 74.4 %all-gather.2.cloned.1.call-done = bf16[256,8192]{0,1:T(8,128)(2,1)} async-done(((bf16[256,2048]{0,1:T(8,128)(2,1)}), bf16[256,8192]{0,1:T(8,128)(2,1)}) %all-gather.2.cloned.1.call-update) | async-done | bytes 4194320 | tf_op jit(solution)/shard_map/all_gather | solution.py:126
  93.6 5.3 %fusion.27 = f32[256,256]{0,1:T(8,128)S(1)} fusion(bf16[256,8192]{0,1:T(8,128)(2,1)} %all-gather.2.cloned.1.call-done, bf16[8192,256]{1,0:T(8,128)(2,1)} %param.11), kind=kOutput, calls=%fused_computation.112 | convolution fusion | flops 1073741824 | bytes 8650752 | tf_op jit(solution)/shard_map/dot_general | solution.py:132
  99.0 5.9 %convolution_convert_fusion.3 = bf16[256,256]{0,1:T(8,128)(2,1)S(1)} fusion(bf16[256,8192]{0,1:T(8,128)(2,1)} %all-gather.2.cloned.1.call-done, bf16[8192,256]{1,0:T(8,128)(2,1)} %param.12), kind=kOutput, calls=%fused_computation.35 | convolution fusion | flops 1073807360 | bytes 8519680 | tf_op jit(solution)/shard_map/dot_general | solution.py:133
  108.6 6.5 %convolution_bitcast_fusion.3 = f32[32,8,8,128]{3,1,2,0:T(8,128)S(1)} fusion(bf16[256,8192]{0,1:T(8,128)(2,1)} %all-gather.2.cloned.1.call-done, bf16[8192,1024]{1,0:T(8,128)(2,1)S(1)} %copy-done), kind=kOutput, calls=%fused_computation.31 | convolution fusion | flops 4294967296 | bytes 22020096 | tf_op jit(solution)/shard_map/dot_general | solution.py:139
  117.0 4.6 all-to-all-start
  125.6 12.9 %fusion.25 = (f32[2,4,256]{2,1,0:T(4,128)S(1)}, f32[2,4,256,2048]{2,3,1,0:T(8,128)}) fusion(pred[256,2048]{0,1:T(8,128)(4,1)} %compare_and_fusion, bf16[2048,2,128,1]{0,2,3,1:T(8,128)(2,1)S(1)} %bitcast.150, bf16[256,2,4,128]{3,0,2,1:T(8,128)(2,1)} %bitcast.156), kind=kOutput, calls=%fused_computation.110 | convolution fusion | flops 1090521088 | bytes 18882560 | tf_op jit(solution)/shard_map/sub | solution.py:156
  138.5 4.3 collective-permute-done.7
  147.6 7.8 %fusion.8 = bf16[2,4,256,2048]{2,3,1,0:T(8,128)(2,1)S(1)} fusion(f32[2,4,256,2048]{2,3,1,0:T(8,128)} %get-tuple-element.64, f32[2,4,256]{2,1,0:T(4,128)S(1)} %get-tuple-element.63), kind=kLoop, calls=%fused_computation.15 | loop fusion | flops 8388608 | bytes 25174016 | tf_op jit(solution)/shard_map/convert_element_type | solution.py:158
  156.7 2.9 copy-done.1
  161.8 6.4 %convolution_convert_fusion = bf16[256,8192]{1,0:T(8,128)(2,1)} fusion(bf16[256,1024]{0,1:T(8,128)(2,1)S(1)} %bitcast.138, bf16[1024,8192]{1,0:T(8,128)(2,1)S(1)} %bitcast.134), kind=kOutput, calls=%fused_computation.9 | convolution fusion | flops 4297064448 | bytes 21495808 | tf_op jit(solution)/shard_map/dot_general | solution.py:163
  168.2 139.2 %collective-permute-done.8 = bf16[2,256,2048]{2,1,0:T(8,128)(2,1)} collective-permute-done((bf16[2,256,2048]{2,1,0:T(8,128)(2,1)}, bf16[2,256,2048]{2,1,0:T(8,128)(2,1)}, u32[]{:S(2)}, u32[]{:S(2)}) %collective-permute-start.8) | collective-permute-done | bytes 2097184 | tf_op jit(solution)/shard_map/ppermute | solution.py:21
  309.4 3.2 reverse_select_fusion
  312.6 6.2 %copy.60 = bf16[2,2,256,2048]{2,3,1,0:T(8,128)(2,1)} copy(bf16[2,2,256,2048]{3,2,1,0:T(8,128)(2,1)} %reverse_select_fusion) | data formatting | bytes 8388608 | tf_op jit(solution)/shard_map/jit(_where)/select_n | solution.py:24
  318.7 6.4 %copy.71 = bf16[256,8,1024]{2,0,1:T(8,128)(2,1)} copy(bf16[256,8,1024]{0,2,1:T(8,128)(2,1)} %bitcast.135) | data formatting | bytes 8388608 | tf_op jit(solution)/shard_map/all_to_all | solution.py:97
  325.2 11.6 %convolution_convert_fusion.2 = bf16[256,1024]{1,0:T(8,128)(2,1)S(1)} fusion(bf16[256,8192]{0,1:T(8,128)(2,1)} %bitcast.136, bf16[1024,8192]{1,0:T(8,128)(2,1)} %param.13), kind=kOutput, calls=%fused_computation.34 | convolution fusion | flops 4295229440 | bytes 21495808 | tf_op jit(solution)/shard_map/dot_general | solution.py:58
  336.8 4.5 all-to-all-start.1
  341.4 6.6 %copy.61 = bf16[8,256,1024]{2,1,0:T(8,128)(2,1)} copy(bf16[8,256,1024]{1,2,0:T(8,128)(2,1)} %bitcast.25) | data formatting | bytes 8388608 | tf_op jit(solution)/shard_map/all_to_all | solution.py:97
  348.4 7.5 %fusion.2 = bf16[2,4,256,2048]{2,3,1,0:T(8,128)(2,1)S(1)} fusion(f32[2,4,256]{2,1,0:T(4,128)S(1)} %bitcast.164, f32[2,4,256,2048]{2,3,1,0:T(8,128)} %get-tuple-element.64, f32[2,4,256]{2,1,0:T(4,128)S(1)} %get-tuple-element.63, bf16[2048,2,128,1]{0,2,3,1:T(8,128)(2,1)} %bitcast.152, bf16[256,2,4,128]{0,3,2,1:T(8,128)(2,1)S(1)} %bitcast.146), kind=kOutput, calls=%fused_computation.3 | convolution fusion | flops 1090519040 | bytes 26755072 | tf_op jit(solution)/shard_map/igrd,jgd->grij/dot_general | solution.py:171
  355.9 3.3 convolution_multiply_fusion
  361.9 6.3 %fusion.13 = bf16[2,128,2048]{2,1,0:T(8,128)(2,1)S(1)} fusion(bf16[256,2,4,128]{0,3,2,1:T(8,128)(2,1)S(1)} %bitcast.147, bf16[2,4,256,2048]{2,3,1,0:T(8,128)(2,1)} %copy-done.1), kind=kOutput, calls=%fused_computation.25 | convolution fusion | flops 1074266112 | bytes 9961472 | tf_op jit(solution)/shard_map/grij,igrd->jgd/dot_general | solution.py:177
  368.3 2.9 fusion.12
  371.4 19.1 %all-to-all-done.1 = bf16[256,8,1024]{2,0,1:T(8,128)(2,1)} async-done(((bf16[256,8,1024]{2,0,1:T(8,128)(2,1)}), bf16[256,8,1024]{2,0,1:T(8,128)(2,1)}, u32[]{:S(2)}, u32[]{:S(2)}) %all-to-all-start.1) | async-done | bytes 4194336 | tf_op jit(solution)/shard_map/all_to_all | solution.py:97
  399.0 19.2 %fusion.20 = f32[256,8192]{1,0:T(8,128)} fusion(bf16[8192,1024]{1,0:T(8,128)(2,1)} %param.10, bf16[32,8,8,128]{3,2,1,0:T(8,128)(2,1)S(1)} %bitcast.144), kind=kOutput, calls=%fused_computation.105 | convolution fusion | flops 4294967296 | bytes 25690112 | tf_op jit(solution)/shard_map/dot_general | solution.py:58
  419.6 6.1 %convolution_add_fusion.1 = f32[256,8192]{1,0:T(8,128)S(1)} fusion(f32[256,8192]{1,0:T(8,128)} %fusion.20, bf16[256,256]{0,1:T(8,128)(2,1)S(1)} %bitcast.159, bf16[8192,256]{1,0:T(8,128)(2,1)} %param.11), kind=kOutput, calls=%fused_computation.8 | convolution fusion | flops 1075838976 | bytes 21102592 | tf_op jit(solution)/shard_map/dot_general | solution.py:58
  425.8 3.4 fusion.4
  432.7 11.4 %collective-permute-done.16 = bf16[256,1024]{0,1:T(8,128)(2,1)S(1)} collective-permute-done((bf16[256,1024]{0,1:T(8,128)(2,1)S(1)}, bf16[256,1024]{0,1:T(8,128)(2,1)S(1)}, u32[]{:S(2)}, u32[]{:S(2)}) %collective-permute-start.16) | collective-permute-done | bytes 524320 | tf_op jit(solution)/shard_map/ppermute | solution.py:71
  444.7 9.0 %collective-permute-done.17 = bf16[256,1024]{0,1:T(8,128)(2,1)S(1)} collective-permute-done((bf16[256,1024]{0,1:T(8,128)(2,1)S(1)}, bf16[256,1024]{0,1:T(8,128)(2,1)S(1)}, u32[]{:S(2)}, u32[]{:S(2)}) %collective-permute-start.17) | collective-permute-done | bytes 524320 | tf_op jit(solution)/shard_map/ppermute | solution.py:71
  463.3 10.0 %fusion.28 = f32[1024,1024]{1,0:T(8,128)} fusion(bf16[2048,1024]{0,1:T(8,128)(2,1)} %copy-done.6, bf16[2048,1024]{1,0:T(8,128)(2,1)} %bitcast.45), kind=kOutput, calls=%fused_computation.113 | convolution fusion | flops 4294967296 | bytes 12582912 | tf_op jit(solution)/shard_map/dot_general | solution.py:64
  473.7 6.4 %collective-permute-done.23 = bf16[256,1536]{1,0:T(8,128)(2,1)S(1)} collective-permute-done((bf16[256,1536]{1,0:T(8,128)(2,1)S(1)}, bf16[256,1536]{1,0:T(8,128)(2,1)S(1)}, u32[]{:S(2)}, u32[]{:S(2)}) %collective-permute-start.23) | collective-permute-done | bytes 786464 | tf_op jit(solution)/shard_map/ppermute | solution.py:71
  480.3 17.2 %collective-permute-done.24 = bf16[256,1536]{1,0:T(8,128)(2,1)S(1)} collective-permute-done((bf16[256,1536]{1,0:T(8,128)(2,1)S(1)}, bf16[256,1536]{1,0:T(8,128)(2,1)S(1)}, u32[]{:S(2)}, u32[]{:S(2)}) %collective-permute-start.24) | collective-permute-done | bytes 786464 | tf_op jit(solution)/shard_map/ppermute | solution.py:71
  500.9 7.1 %convolution_bitcast_fusion = f32[1024,1536]{0,1:T(8,128)S(1)} fusion(bf16[2048,1536]{1,0:T(8,128)(2,1)S(1)} %constant_dynamic-update-slice_fusion.24, bf16[2048,1024]{1,0:T(8,128)(2,1)S(1)} %bitcast.149), kind=kOutput, calls=%fused_computation.17 | convolution fusion | flops 6442450944 | bytes 16777216 | tf_op jit(solution)/shard_map/dot_general | solution.py:64
  513.3 5.3 %copy.74 = f32[1024,1024]{1,0:T(8,128)} copy(f32[1024,1024]{0,1:T(8,128)} %slice.105) | data formatting | bytes 8388608
  (180 shorter events, 71.2 us)
Async XLA Ops:
  7.2 86.5 %all-gather.2.cloned.1.call-start = ((), (), s32[]{:S(2)}) async-start(), calls=%async_computation.4 | async-start | bytes 5242880 | tf_op jit(solution)/shard_map/all_gather | solution.py:126
  105.0 16.8 %collective-permute-start = (bf16[256,512]{0,1:T(8,128)(2,1)S(1)}, bf16[256,512]{0,1:T(8,128)(2,1)S(1)}, u32[]{:S(2)}, u32[]{:S(2)}) collective-permute-start(bf16[256,512]{0,1:T(8,128)(2,1)S(1)} %get-tuple-element.59), channel_id=1, source_target_pairs={{0,8},{4,12},{8,0},{12,4},{16,24},{20,28},{24,16},{28,20},{1,9},{5... | collective-permute-start | bytes 786440 | tf_op jit(solution)/shard_map/ppermute | solution.py:71
  106.6 15.7 %collective-permute-start.1 = (bf16[256,512]{0,1:T(8,128)(2,1)S(1)}, bf16[256,512]{0,1:T(8,128)(2,1)S(1)}, u32[]{:S(2)}, u32[]{:S(2)}) collective-permute-start(bf16[256,512]{0,1:T(8,128)(2,1)S(1)} %get-tuple-element.59), channel_id=1, source_target_pairs={{0,16},{4,20},{8,24},{12,28},{16,0},{20,4},{24,8},{28,12},{1,17},{... | collective-permute-start | bytes 786440 | tf_op jit(solution)/shard_map/ppermute | solution.py:71
  108.1 14.4 %collective-permute-start.2 = (bf16[256,512]{0,1:T(8,128)(2,1)S(1)}, bf16[256,512]{0,1:T(8,128)(2,1)S(1)}, u32[]{:S(2)}, u32[]{:S(2)}) collective-permute-start(bf16[256,512]{0,1:T(8,128)(2,1)S(1)} %get-tuple-element.59), channel_id=1, source_target_pairs={{0,24},{4,28},{8,16},{12,20},{16,8},{20,12},{24,0},{28,4},{1,25},{... | collective-permute-start | bytes 786440 | tf_op jit(solution)/shard_map/ppermute | solution.py:71
  108.6 14.5 %collective-permute-start.3 = (bf16[256,512]{0,1:T(8,128)(2,1)S(1)}, bf16[256,512]{0,1:T(8,128)(2,1)}, u32[]{:S(2)}, u32[]{:S(2)}) collective-permute-start(bf16[256,512]{0,1:T(8,128)(2,1)S(1)} %get-tuple-element.59), channel_id=1, source_target_pairs={{0,4},{4,0},{8,12},{12,8},{16,20},{20,16},{24,28},{28,24},{1,5},{5... | collective-permute-start | bytes 786440 | tf_op jit(solution)/shard_map/ppermute | solution.py:71
  117.0 25.9 %collective-permute-start.7 = (bf16[1,256,2048]{2,1,0:T(8,128)(2,1)}, bf16[1,256,2048]{2,1,0:T(8,128)(2,1)}, u32[]{:S(2)}, u32[]{:S(2)}) collective-permute-start(bf16[1,256,2048]{2,1,0:T(8,128)(2,1)} %bitcast.16), channel_id=1, source_target_pairs={{0,1},{1,0},{2,3},{3,2},{4,5},{5,4},{6,7},{7,6},{8,9},{9,8},{10,11... | collective-permute-start | bytes 3145736 | tf_op jit(solution)/shard_map/ppermute | solution.py:21
  117.0 219.8 %all-to-all-start = ((bf16[256,8,1024]{0,2,1:T(8,128)(2,1)}), bf16[256,8,1024]{0,2,1:T(8,128)(2,1)}, u32[]{:S(2)}, u32[]{:S(2)}) async-start(bf16[256,8,1024]{0,2,1:T(8,128)(2,1)} %bitcast.132), calls=%async_computation.1 | async-start | bytes 8388608 | tf_op jit(solution)/shard_map/all_to_all | solution.py:97
  121.5 401.4 %reduce-scatter.3.cloned.1.call-start = ((), (), s32[]{:S(2)}) async-start(), calls=%async_computation.5 | async-start | bytes 5242880 | tf_op jit(solution)/shard_map/reduce_scatter | solution.py:164
  121.8 2.3 collective-permute-start.4
  146.6 160.8 %collective-permute-start.8 = (bf16[2,256,2048]{2,1,0:T(8,128)(2,1)}, bf16[2,256,2048]{2,1,0:T(8,128)(2,1)}, u32[]{:S(2)}, u32[]{:S(2)}) collective-permute-start(bf16[2,256,2048]{2,1,0:T(8,128)(2,1)} %get-tuple-element.48), channel_id=1, source_target_pairs={{0,2},{1,3},{2,0},{3,1},{4,6},{5,7},{6,4},{7,5},{8,10},{9,11},{10,... | collective-permute-start | bytes 6291464 | tf_op jit(solution)/shard_map/ppermute | solution.py:21
  336.8 53.7 %all-to-all-start.1 = ((bf16[256,8,1024]{2,0,1:T(8,128)(2,1)}), bf16[256,8,1024]{2,0,1:T(8,128)(2,1)}, u32[]{:S(2)}, u32[]{:S(2)}) async-start(bf16[256,8,1024]{2,0,1:T(8,128)(2,1)} %copy.71), calls=%async_computation.2 | async-start | bytes 8388608 | tf_op jit(solution)/shard_map/all_to_all | solution.py:97
  341.3 181.6 %reduce-scatter.5.cloned.1.call-start = ((), (), s32[]{:S(2)}) async-start(), calls=%async_computation.6 | async-start | bytes 5242880 | tf_op jit(solution)/shard_map/reduce_scatter | solution.py:189
  391.2 3.2 collective-permute-start.10
  391.2 3.2 collective-permute-start.14
  391.8 2.7 collective-permute-start.12
  393.9 24.3 %collective-permute-start.9 = (bf16[256,512]{0,1:T(8,128)(2,1)}, bf16[256,512]{0,1:T(8,128)(2,1)S(1)}, u32[]{:S(2)}, u32[]{:S(2)}) collective-permute-start(bf16[256,512]{0,1:T(8,128)(2,1)} %get-tuple-element.40), channel_id=1, source_target_pairs={{0,4},{4,0},{8,12},{12,8},{16,20},{20,16},{24,28},{28,24},{1,5},{5... | collective-permute-start | bytes 786440 | tf_op jit(solution)/shard_map/ppermute | solution.py:71
  395.5 22.7 %collective-permute-start.15 = (bf16[256,512]{0,1:T(8,128)(2,1)}, bf16[256,512]{0,1:T(8,128)(2,1)}, u32[]{:S(2)}, u32[]{:S(2)}) collective-permute-start(bf16[256,512]{0,1:T(8,128)(2,1)} %get-tuple-element.45), channel_id=1, source_target_pairs={{0,24},{4,28},{8,16},{12,20},{16,8},{20,12},{24,0},{28,4},{1,25},{... | collective-permute-start | bytes 786440 | tf_op jit(solution)/shard_map/ppermute | solution.py:71
  396.1 22.2 %collective-permute-start.13 = (bf16[256,512]{0,1:T(8,128)(2,1)}, bf16[256,512]{0,1:T(8,128)(2,1)}, u32[]{:S(2)}, u32[]{:S(2)}) collective-permute-start(bf16[256,512]{0,1:T(8,128)(2,1)} %get-tuple-element.46), channel_id=1, source_target_pairs={{0,16},{4,20},{8,24},{12,28},{16,0},{20,4},{24,8},{28,12},{1,17},{... | collective-permute-start | bytes 786440 | tf_op jit(solution)/shard_map/ppermute | solution.py:71
  397.4 20.8 %collective-permute-start.11 = (bf16[256,512]{0,1:T(8,128)(2,1)}, bf16[256,512]{0,1:T(8,128)(2,1)}, u32[]{:S(2)}, u32[]{:S(2)}) collective-permute-start(bf16[256,512]{0,1:T(8,128)(2,1)} %get-tuple-element.44), channel_id=1, source_target_pairs={{0,8},{4,12},{8,0},{12,4},{16,24},{20,28},{24,16},{28,20},{1,9},{5... | collective-permute-start | bytes 786440 | tf_op jit(solution)/shard_map/ppermute | solution.py:71
  429.2 14.9 %collective-permute-start.16 = (bf16[256,1024]{0,1:T(8,128)(2,1)S(1)}, bf16[256,1024]{0,1:T(8,128)(2,1)S(1)}, u32[]{:S(2)}, u32[]{:S(2)}) collective-permute-start(bf16[256,1024]{0,1:T(8,128)(2,1)S(1)} %bitcast.139), channel_id=1, source_target_pairs={{0,8},{4,12},{8,0},{12,4},{16,24},{20,28},{24,16},{28,20},{1,9},{5... | collective-permute-start | bytes 1572872 | tf_op jit(solution)/shard_map/ppermute | solution.py:71
  429.8 24.0 %collective-permute-start.17 = (bf16[256,1024]{0,1:T(8,128)(2,1)S(1)}, bf16[256,1024]{0,1:T(8,128)(2,1)S(1)}, u32[]{:S(2)}, u32[]{:S(2)}) collective-permute-start(bf16[256,1024]{0,1:T(8,128)(2,1)S(1)} %bitcast.140), channel_id=1, source_target_pairs={{0,16},{4,20},{8,24},{12,28},{16,0},{20,4},{24,8},{28,12},{1,17},{... | collective-permute-start | bytes 1572872 | tf_op jit(solution)/shard_map/ppermute | solution.py:71
  430.4 23.4 %collective-permute-start.18 = (bf16[256,1024]{0,1:T(8,128)(2,1)S(1)}, bf16[256,1024]{0,1:T(8,128)(2,1)S(1)}, u32[]{:S(2)}, u32[]{:S(2)}) collective-permute-start(bf16[256,1024]{0,1:T(8,128)(2,1)S(1)} %bitcast.141), channel_id=1, source_target_pairs={{0,24},{4,28},{8,16},{12,20},{16,8},{20,12},{24,0},{28,4},{1,25},{... | collective-permute-start | bytes 1572872 | tf_op jit(solution)/shard_map/ppermute | solution.py:71
  432.7 21.8 %collective-permute-start.19 = (bf16[256,1024]{0,1:T(8,128)(2,1)S(1)}, bf16[256,1024]{0,1:T(8,128)(2,1)S(1)}, u32[]{:S(2)}, u32[]{:S(2)}) collective-permute-start(bf16[256,1024]{0,1:T(8,128)(2,1)S(1)} %bitcast.142), channel_id=1, source_target_pairs={{0,4},{4,0},{8,12},{12,8},{16,20},{20,16},{24,28},{28,24},{1,5},{5... | collective-permute-start | bytes 1572872 | tf_op jit(solution)/shard_map/ppermute | solution.py:71
  444.1 10.5 %collective-permute-start.20 = (bf16[256,1024]{0,1:T(8,128)(2,1)S(1)}, bf16[256,1024]{0,1:T(8,128)(2,1)S(1)}, u32[]{:S(2)}, u32[]{:S(2)}) collective-permute-start(bf16[256,1024]{0,1:T(8,128)(2,1)S(1)} %collective-permute-done.16), channel_id=1, source_target_pairs={{0,4},{4,0},{8,12},{12,8},{16,20},{20,16},{24,28},{28,24},{1,5},{5... | collective-permute-start | bytes 1572872 | tf_op jit(solution)/shard_map/ppermute | solution.py:71
  453.8 2.6 collective-permute-start.22
  459.7 20.4 %collective-permute-start.23 = (bf16[256,1536]{1,0:T(8,128)(2,1)S(1)}, bf16[256,1536]{1,0:T(8,128)(2,1)S(1)}, u32[]{:S(2)}, u32[]{:S(2)}) collective-permute-start(bf16[256,1536]{1,0:T(8,128)(2,1)S(1)} %pad_maximum_fusion.3), channel_id=1, source_target_pairs={{0,8},{4,12},{8,0},{12,4},{16,24},{20,28},{24,16},{28,20},{1,9},{5... | collective-permute-start | bytes 2359304 | tf_op jit(solution)/shard_map/ppermute | solution.py:71
  461.3 36.2 %collective-permute-start.24 = (bf16[256,1536]{1,0:T(8,128)(2,1)S(1)}, bf16[256,1536]{1,0:T(8,128)(2,1)S(1)}, u32[]{:S(2)}, u32[]{:S(2)}) collective-permute-start(bf16[256,1536]{1,0:T(8,128)(2,1)S(1)} %pad_maximum_fusion.3), channel_id=1, source_target_pairs={{0,16},{4,20},{8,24},{12,28},{16,0},{20,4},{24,8},{28,12},{1,17},{... | collective-permute-start | bytes 2359304 | tf_op jit(solution)/shard_map/ppermute | solution.py:71
  461.8 35.7 %collective-permute-start.25 = (bf16[256,1536]{1,0:T(8,128)(2,1)S(1)}, bf16[256,1536]{1,0:T(8,128)(2,1)S(1)}, u32[]{:S(2)}, u32[]{:S(2)}) collective-permute-start(bf16[256,1536]{1,0:T(8,128)(2,1)S(1)} %pad_maximum_fusion.3), channel_id=1, source_target_pairs={{0,24},{4,28},{8,16},{12,20},{16,8},{20,12},{24,0},{28,4},{1,25},{... | collective-permute-start | bytes 2359304 | tf_op jit(solution)/shard_map/ppermute | solution.py:71
  473.3 24.9 %collective-permute-start.26 = (bf16[256,1536]{1,0:T(8,128)(2,1)S(1)}, bf16[256,1536]{1,0:T(8,128)(2,1)S(1)}, u32[]{:S(2)}, u32[]{:S(2)}) collective-permute-start(bf16[256,1536]{1,0:T(8,128)(2,1)S(1)} %pad_maximum_fusion.3), channel_id=1, source_target_pairs={{0,4},{4,0},{8,12},{12,8},{16,20},{20,16},{24,28},{28,24},{1,5},{5... | collective-permute-start | bytes 2359304 | tf_op jit(solution)/shard_map/ppermute | solution.py:71
  480.2 18.1 %collective-permute-start.27 = (bf16[256,1536]{1,0:T(8,128)(2,1)S(1)}, bf16[256,1536]{1,0:T(8,128)(2,1)S(1)}, u32[]{:S(2)}, u32[]{:S(2)}) collective-permute-start(bf16[256,1536]{1,0:T(8,128)(2,1)S(1)} %collective-permute-done.23), channel_id=1, source_target_pairs={{0,4},{4,0},{8,12},{12,8},{16,20},{20,16},{24,28},{28,24},{1,5},{5... | collective-permute-start | bytes 2359304 | tf_op jit(solution)/shard_map/ppermute | solution.py:71
  497.5 2.3 collective-permute-start.28
  497.5 3.3 collective-permute-start.29
  (19 other events, 124.6 us)
Sparse Core Ops, SparseCore 0:
  10.1 83.4 all-gather.1
  168.3 114.1 reduce-scatter.2
  429.3 73.3 reduce-scatter.4
